TPU v7x, 256 devices: a whole 4x4x8 slice. The times are simulated.
256 devices in a mesh: leaf: 32 (over x, z), rows: 8 (over y, core).
Axes of the slice: x: 4, y: 4, z: 8, core: 2. Of those that a mesh axis runs over, the one named last changes fastest.
Arguments:
- leaf_basis: float32 [8192, 64, 256], P(('leaf', 'rows')), may hold values from -0.375 to 0.375
- leaf_transfer: float32 [8192, 64, 64], P(('leaf', 'rows'))
- device_transfer: float32 [256, 64, 64], P(('leaf', 'rows'))
- upper_transfer: float32 [254, 64, 64], replicated
- couplings: float32 [8192, 64, 64], P(('leaf', 'rows')), may hold values from -0.1875 to 0.1875
- couple_offset: int32 [8192], P(('leaf', 'rows')), may hold values from 8 to 248, as said below
Outputs:
- leaf_orth: float32 [8192, 64, 256], P(('leaf', 'rows'))
- leaf_bridge: float32 [8192, 64, 64], P(('leaf', 'rows'))
- new_transfers: float32 [256, 8, 64, 64], P(('leaf', 'rows'))
- coupled: float32 [8192, 64, 64], P(('leaf', 'rows'))
Inputs may be any that keep to these rules, and one draw needn't show every extreme that they name: couple_offset[b] is 8 times a number of 1 to 31, so block b couples device cluster b // 32 with a cluster of another branch at the same position within its branch; among the 32 blocks of one device cluster, at most 2 name the same column cluster, and on every device some column cluster is named exactly 2 times.
All inputs are finite; a program needn't handle non-finite values.
Results may differ from a plain program's by a relative error of at most 0.0001.
Values sent between devices are 32-bit elements; how exact they have to be, the bound alone decides.
A program may use at most 128 MiB of HBM per device.

v0:
```python
import jax
import jax.numpy as jnp
from jax import lax
from jax.sharding import PartitionSpec as P

HIGH = lax.Precision.HIGHEST


def swapped(value, axis, apart):
    mask = 2**apart
    pairs = [(source, source ^ mask) for source in range(lax.axis_size(axis))]
    return lax.ppermute(value, axis, pairs)


def lower_solve(low, right):
    return lax.linalg.triangular_solve(low, right, left_side=True, lower=True)


def lift(grams, trans):
    inner = jnp.einsum("nkl,nlj->nkj", grams, trans, precision=HIGH)
    return jnp.einsum("nki,nkj->nij", trans, inner, precision=HIGH)


def per_device(
    leaf_basis, leaf_transfer, device_transfer, upper_transfer, couplings, couple_offset
):
    n_rows = lax.axis_size("rows")
    n_leaf = lax.axis_size("leaf")
    row_bits = n_rows.bit_length() - 1
    leaf_bits = n_leaf.bit_length() - 1
    levels = row_bits + leaf_bits
    clusters = n_rows * n_leaf
    branch = lax.axis_index("leaf")
    row_id = lax.axis_index("rows")
    myself = branch * n_rows + row_id
    leaf_gram = jnp.einsum("nrk,nsk->nrs", leaf_basis, leaf_basis, precision=HIGH)
    leaf_low = jnp.linalg.cholesky(leaf_gram)
    leaf_orth = lower_solve(leaf_low, leaf_basis)
    own_gram = jnp.sum(lift(leaf_gram, leaf_transfer), axis=0)
    own_lift = lift(own_gram[None], device_transfer)
    row_grams, row_lifts = (
        lax.all_gather(own_gram[None], "rows", axis=0, tiled=True),
        lax.all_gather(own_lift, "rows", axis=0, tiled=True),
    )
    path = [own_gram]
    lifted = row_lifts
    level = levels
    start = branch * n_rows
    for step in range(row_bits):
        gram = lifted[0::2] + lifted[1::2]
        level -= 1
        start = start // 2
        path.append(lax.dynamic_index_in_dim(gram, row_id >> step + 1, 0, keepdims=False))
        trans = lax.dynamic_slice_in_dim(upper_transfer, 2**level - 2 + start, gram.shape[0], 0)
        lifted = lift(gram, trans)
    blocks = couplings.shape[0]
    targets = (myself + couple_offset) % clusters
    column_grams = None
    carry = lifted[0]
    for bit in range(leaf_bits):
        gram = carry + swapped(carry, "leaf", bit)
        level -= 1
        path.append(gram)
        if level > 0:
            node = branch >> bit + 1
            trans = lax.dynamic_slice_in_dim(upper_transfer, 2**level - 2 + node, 1, 0)
            carry = lift(gram[None], trans)[0]
    piece = lax.all_gather(row_grams, "leaf", axis=0, tiled=True)
    labels = lax.broadcasted_iota(jnp.int32, (blocks, piece.shape[0]), 1)
    onehot = (targets[:, None] == labels).astype(jnp.float32)
    column_grams = jnp.einsum("bp,pij->bij", onehot, piece, precision=HIGH)
    lows = jnp.linalg.cholesky(jnp.stack(path, axis=0))
    edges = [device_transfer[0]]
    for step in range(1, levels):
        node_level = levels - step
        edges.append(
            lax.dynamic_index_in_dim(
                upper_transfer, 2**node_level - 2 + (myself >> step), 0, keepdims=False
            )
        )
    edge_stack = jnp.stack(edges, axis=0)
    right = jnp.einsum("nki,nkj->nij", edge_stack, lows[:levels], precision=HIGH)
    fresh = jnp.swapaxes(lower_solve(lows[1:], right), 1, 2)
    new_transfers = fresh[None]
    device_low = jnp.broadcast_to(lows[0], leaf_transfer.shape)
    bridge_right = jnp.einsum("nki,nkj->nij", leaf_transfer, leaf_low, precision=HIGH)
    leaf_bridge = jnp.swapaxes(lower_solve(device_low, bridge_right), 1, 2)
    column_low = jnp.linalg.cholesky(column_grams)
    inner = jnp.einsum("nkl,nlj->nkj", couplings, column_low, precision=HIGH)
    coupled = jnp.einsum("ki,nkj->nij", lows[0], inner, precision=HIGH)
    return (leaf_orth, leaf_bridge, new_transfers, coupled)


def solution(mesh):
    in_specs = (
        P(("leaf", "rows"), None, None),
        P(("leaf", "rows"), None, None),
        P(("leaf", "rows"), None, None),
        P(),
        P(("leaf", "rows"), None, None),
        P(("leaf", "rows")),
    )
    out_specs = (
        P(("leaf", "rows"), None, None),
        P(("leaf", "rows"), None, None),
        P(("leaf", "rows"), None, None, None),
        P(("leaf", "rows"), None, None),
    )
    return jax.shard_map(
        per_device, mesh=mesh, in_specs=in_specs, out_specs=out_specs, check_vma=False
    )
```

profile of v0, /device:TPU:8, one launch (start us, length us, event | category | flops | bytes accessed | tf_op | source)
XLA Modules:
  0.0 826.6 jit_solution(12771305629167005888)
XLA Ops:
  7.3 18.5 %constant_dynamic-slice_fusion = (f32[1,64,64]{0,2,1:T(8,128)}, f32[1,64,64]{0,2,1:T(8,128)}, f32[1,64,64]{0,2,1:T(8,128)}, f32[1,64,64]{0,2,1:T(8,128)}, f32[1,...) fusion(f32[254,64,64]{0,2,1:T(8,128)} %param.10, ...), kind=kLoop, calls=%fused_computation.88 | loop fusion | bytes 393264 | tf_op jit(solution)/shard_map/jit(dynamic_index_in_dim)/dynamic_slice | solution.py:77
  28.1 4.1 constant_dynamic-slice_fusion.13
  32.2 2.9 copy.256
  42.2 13.0 %all-gather = f32[512,64]{1,0:T(8,128)S(1)} all-gather(f32[64,64]{1,0:T(8,128)S(1)} %copy.185), channel_id=2, replica_groups=mesh['leaf'=32,'rows'=8] {'rows'}, dimensions={0}, use_global_device_ids=true | all-gather | bytes 147456 | tf_op jit(solution)/shard_map/all_gather | solution.py:43
  64.1 4.1 constant_dynamic-slice_fusion.12
  75.8 12.8 %all-gather.1 = f32[512,64]{1,0:T(8,128)S(1)} all-gather(f32[64,64]{1,0:T(8,128)S(1)} %copy.226), channel_id=3, replica_groups=mesh['leaf'=32,'rows'=8] {'rows'}, dimensions={0}, use_global_device_ids=true | all-gather | bytes 147456 | tf_op jit(solution)/shard_map/all_gather | solution.py:42
  93.2 2.9 copy.263
  96.0 2.9 copy.264
  98.9 2.9 copy.265
  101.8 2.9 copy.266
  104.7 2.9 copy.267
  107.6 2.9 copy.268
  110.5 2.9 copy.269
  113.4 188.6 %custom-call.21 = f32[32,64,64]{2,1,0:T(8,128)S(1)} custom-call(f32[32,64,64]{2,1,0:T(8,128)} %fusion.1), custom_call_target="Cholesky" | custom-call | tf_op jit(solution)/shard_map/jit(cholesky)/cholesky | solution.py:37
  306.2 2.8 select_bitcast_fusion
  309.0 3.9 copy.183
  312.9 68.5 %custom-call.16 = f32[32,1,64,64]{0,2,3,1:T(8,128)} custom-call(f32[32,1,64,64]{0,3,2,1:T(8,128)} %get-tuple-element.25), custom_call_target="InvertDiagBlocksLowerTriangular" | custom-call | tf_op jit(solution)/shard_map/triangular_solve | solution.py:16
  381.5 3.9 copy.182
  397.0 3.4 fusion.54
  400.4 3.2 fusion.53
  414.6 3.4 collective-permute-start.1
  420.8 6.4 collective-permute-start.2
  434.1 3.1 collective-permute-start.4
  439.8 52.8 %custom-call.17 = f32[9,64,64]{2,1,0:T(8,128)S(1)} custom-call(f32[9,64,64]{2,1,0:T(8,128)S(1)} %fusion.8), custom_call_target="Cholesky" | custom-call | tf_op jit(solution)/shard_map/jit(cholesky)/cholesky | solution.py:72
  492.8 40.0 %custom-call.19 = f32[8,1,64,64]{2,3,1,0:T(8,128)} custom-call(f32[8,1,64,64]{3,2,1,0:T(8,128)S(1)} %fusion.9), custom_call_target="InvertDiagBlocksLowerTriangular" | custom-call | tf_op jit(solution)/shard_map/triangular_solve | solution.py:16
  535.4 68.5 %custom-call.18 = f32[32,1,64,64]{0,2,3,1:T(8,128)} custom-call(f32[32,1,64,64]{0,3,2,1:T(8,128)} %broadcast_select_fusion), custom_call_target="InvertDiagBlocksLowerTriangular" | custom-call | tf_op jit(solution)/shard_map/triangular_solve | solution.py:16
  603.9 4.0 copy.215
  611.6 2.8 fusion.60
  614.3 6.5 fusion.40
  622.5 2.9 fusion
  625.3 188.4 %custom-call.22 = f32[32,64,64]{2,1,0:T(8,128)S(1)} custom-call(f32[32,64,64]{2,1,0:T(8,128)} %fusion), custom_call_target="Cholesky" | custom-call | tf_op jit(solution)/shard_map/jit(cholesky)/cholesky | solution.py:88
  814.0 3.2 convolution_bitcast_fusion.1
  (112 shorter events, 80.1 us)
Async XLA Ops:
  7.2 28.0 %copy-start = (f32[32,64,256]{2,1,0:T(8,128)S(1)}, f32[32,64,256]{2,1,0:T(8,128)}, u32[]{:S(2)}) copy-start(f32[32,64,256]{2,1,0:T(8,128)} %param.7) | copy-start | bytes 6291460
  7.2 607.2 %all-gather.4.cloned.1.call-start = ((), (), s32[]{:S(2)}) async-start(), calls=%async_computation | async-start | bytes 8650752 | tf_op jit(solution)/shard_map/all_gather | solution.py:68
  35.1 2.1 copy-start.2
  37.2 3.1 copy-start.11
  40.3 23.8 %copy-start.10 = (f32[64,64,1]{1,0,2:T(8,128)}, f32[64,64,1]{1,0,2:T(8,128)S(1)}, u32[]{:S(2)}) copy-start(f32[64,64,1]{1,0,2:T(8,128)S(1)} %get-tuple-element.42) | copy-start | bytes 49156
  60.2 0.7 copy-start.7
  71.9 0.6 copy-start.9
  73.6 339.8 %collective-permute-start = (f32[64,64]{0,1:T(8,128)}, f32[64,64]{0,1:T(8,128)}, u32[]{:S(2)}, u32[]{:S(2)}) collective-permute-start(f32[64,64]{0,1:T(8,128)} %fusion.32), channel_id=1, source_target_pairs={{0,8},{8,0},{16,24},{24,16},{32,40},{40,32},{48,56},{56,48},{64,72... | collective-permute-start | bytes 49160 | tf_op jit(solution)/shard_map/ppermute | solution.py:12
  304.0 2.2 copy-start.1
  312.9 72.4 %copy-start.12 = (f32[1,64,64]{2,1,0:T(8,128)S(1)}, f32[1,64,64]{2,1,0:T(8,128)}, u32[]{:S(2)}) copy-start(f32[1,64,64]{2,1,0:T(8,128)} %param.9) | copy-start | bytes 49156
  312.9 73.8 %copy-start.8 = (f32[2,64,64]{1,2,0:T(8,128)S(1)}, f32[2,64,64]{1,2,0:T(8,128)}, u32[]{:S(2)}) copy-start(f32[2,64,64]{1,2,0:T(8,128)} %slice_add_fusion) | copy-start | bytes 98308
  312.9 84.1 %copy-start.3 = (f32[32,64,64]{2,1,0:T(8,128)S(1)}, f32[32,64,64]{2,1,0:T(8,128)}, u32[]{:S(2)}) copy-start(f32[32,64,64]{2,1,0:T(8,128)} %param.8) | copy-start | bytes 1572868
  385.4 15.0 %copy-start.5 = (f32[32,64,64]{2,1,0:T(8,128)S(1)}, f32[32,64,64]{2,1,0:T(8,128)}, u32[]{:S(2)}) copy-start(f32[32,64,64]{2,1,0:T(8,128)} %copy.182) | copy-start | bytes 1572868
  400.4 3.2 copy-start.13
  414.6 5.6 collective-permute-start.1
  420.8 8.3 %collective-permute-start.2 = (f32[64,64]{0,1:T(8,128)S(1)}, f32[64,64]{0,1:T(8,128)S(1)}, u32[]{:S(2)}, u32[]{:S(2)}) collective-permute-start(f32[64,64]{0,1:T(8,128)S(1)} %fusion.22), channel_id=1, source_target_pairs={{0,32},{8,40},{16,48},{24,56},{32,0},{40,8},{48,16},{56,24},{64,96... | collective-permute-start | bytes 49160 | tf_op jit(solution)/shard_map/ppermute | solution.py:12
  429.6 4.0 collective-permute-start.3
  434.1 5.5 collective-permute-start.4
  603.9 7.7 copy-start.4
  607.9 3.7 copy-start.6
  609.5 4.8 copy-start.14
Sparse Core Ops, SparseCore 0:
  89.6 105.7 all-gather.3
where the time goes:
time: 837 us; the launch traced here: 827 us
  other arithmetic  625 us (75%)
  local copies, waits for them, and re-layouts  99.8 us (12%)
  matrix products  37.7 us (5%)
  blocking collectives  25.8 us (3%)
  starting transfers between devices  15.8 us (2%)
  between operations  14.7 us (2%)
    another operation x4, other arithmetic, per_device(): leaf_low = jnp.linalg.cholesky(leaf_gram)  191 us
    another operation x3, other arithmetic, per_device(): column_low = jnp.linalg.cholesky(column_grams)  189 us
    another operation x7, other arithmetic, lower_solve(): return lax.linalg.triangular_solve(low, right, left_side=True, lower=True)  182 us
    another operation x4, other arithmetic, per_device(): lows = jnp.linalg.cholesky(jnp.stack(path, axis=0))  52.9 us
    unnamed x56, local copies, waits for them, and re-layouts  52.4 us
    dynamic_slice x1, local copies, waits for them, and re-layouts, per_device(): lax.dynamic_index_in_dim(upper_transfer, 2 ** node_level - 2 + (myself >>...  18.5 us
  transfers between devices with their start and end apart: 6, of which 4 were waited for; matrix products, arithmetic and copies ran while one was open for 61% of the time, Pallas kernels for 0%

commit v1 on v0

v1 whole, which is shorter than its diff:
```python
import functools

import jax
import jax.numpy as jnp
from jax import lax
from jax.experimental import pallas as pl
from jax.experimental.pallas import tpu as pltpu
from jax.sharding import PartitionSpec as P

HIGH = lax.Precision.HIGHEST
RANK = 64
Z_BITS = 3


def mm(a, b, dims="nn"):
    contract = ((1 if dims[0] == "n" else 0,), (0 if dims[1] == "n" else 1,))
    return lax.dot_general(
        a, b, (contract, ((), ())), precision=HIGH, preferred_element_type=jnp.float32
    )


def lift(gram, trans):
    return mm(trans, mm(gram, trans), "tn")


def pack(a):
    return jnp.concatenate([a[: RANK // 2], a[RANK // 2 :]], axis=1)


def unpack(a):
    return jnp.concatenate([a[:, :RANK], a[:, RANK:]], axis=0)


def eliminate(m, pairs, first, last):
    lane = lax.broadcasted_iota(jnp.int32, (1, 1, 128), 2) & (RANK - 1)
    for base in range(first, last, 8):
        rows = RANK - base
        sub = lax.broadcasted_iota(jnp.int32, (1, rows, 1), 1) + base
        half = lax.broadcasted_iota(jnp.int32, (pairs * rows, 128), 1) & RANK

        def step(k, carry, base=base, rows=rows, sub=sub, half=half):
            here = lane == k
            row = m[0:pairs, pl.ds(k, 1), :]
            tail = m[0:pairs, base:RANK, :]
            column = jnp.take_along_axis(
                tail.reshape(pairs * rows, 128), half + k, axis=1, mode="promise_in_bounds"
            ).reshape(pairs, rows, 128)
            pivot = jnp.take_along_axis(
                jnp.broadcast_to(row, (pairs, 8, 128)).reshape(pairs * 8, 128),
                half[: pairs * 8] + k,
                axis=1,
                mode="promise_in_bounds",
            ).reshape(pairs, 8, 128)[:, :1]
            scale = lax.rsqrt(pivot)
            scaled = jnp.where(here, 1.0, row) * scale
            fresh = jnp.where(here, 0.0, tail) - column * (scaled * scale)
            m[0:pairs, base:RANK, :] = jnp.where(
                sub > k, fresh, jnp.where(sub == k, scaled, tail)
            )
            return carry

        lax.fori_loop(base, base + 8, step, 0)


def triangles(a):
    row = lax.broadcasted_iota(jnp.int32, (RANK, RANK), 0)
    col = lax.broadcasted_iota(jnp.int32, (RANK, RANK), 1)
    upper = jnp.where(col > row, a, jnp.where(col == row, 1.0 / a, 0.0))
    inverse = jnp.where(col <= row, a, 0.0)
    return upper, inverse


def tree_kernel(
    row_bits, x_bits,
    basis, transfer, device_transfer, upper_transfer,
    leaf_out, path_out, low_out, edge_out,
    state, path, edge, nodes, total,
    row_buf, z_buf, x_buf, lows, mine,
    edge_sem, row_send, row_recv, z_send, z_recv, x_send, x_recv,
    zl_send, zl_recv, xl_send, xl_recv,
):
    n_rows, n_z, n_x = 2**row_bits, 2**Z_BITS, 2**x_bits
    levels = row_bits + Z_BITS + x_bits
    branch = lax.axis_index("leaf")
    row_id = lax.axis_index("rows")
    x_id = branch // n_z
    z_id = branch % n_z
    leaves = basis.shape[0]
    pairs = leaves // 2

    def to_row(d):
        return {"rows": (row_id + d) % n_rows}

    def to_z(d):
        return {"leaf": x_id * n_z + (z_id + d) % n_z}

    def to_x(d):
        return {"leaf": ((x_id + d) % n_x) * n_z + z_id}

    barrier = pltpu.get_barrier_semaphore()
    for place, count in ((to_row, n_rows), (to_z, n_z), (to_x, n_x)):
        for d in range(1, count):
            pl.semaphore_signal(
                barrier, inc=1, device_id=place(d), device_id_type=pl.DeviceIdType.MESH
            )

    spans = []
    at = 0
    start = branch * n_rows
    count = n_rows
    level = levels
    for bits, begin in ((row_bits, branch), (Z_BITS, x_id), (x_bits, 0)):
        for step in range(bits):
            level -= 1
            count = 2 ** (bits - 1 - step)
            spans.append((at, count, level, 2**level - 2 + begin * count))
            at += count
    fetches = []
    for index, (at, count, level, source) in enumerate(spans):
        if level > 0:
            fetch = pltpu.make_async_copy(
                upper_transfer.at[pl.ds(source, count)],
                nodes.at[pl.ds(at, count)],
                edge_sem.at[index],
            )
            fetch.start()
            fetches.append(fetch)

    total[...] = jnp.zeros_like(total)

    def leaf_pair(p, carry):
        part = None
        grams = []
        for h in range(2):
            b = basis[2 * p + h]
            gram = mm(b, b, "nt")
            trans = transfer[2 * p + h]
            moved = mm(trans, mm(gram, trans), "tn")
            part = moved if part is None else part + moved
            grams.append(gram)
        state[p] = jnp.concatenate(grams, axis=1)
        total[...] += part
        return carry

    lax.fori_loop(0, pairs, leaf_pair, 0)
    own = total[...]
    state[pairs] = jnp.concatenate([own, own], axis=1)
    edge[0] = device_transfer[0]
    row_buf[row_id] = pack(lift(own, device_transfer[0]))
    pl.semaphore_wait(barrier, n_rows - 1 + n_z - 1 + n_x - 1)

    def sends(buf, slot, place, count, send, recv):
        out = []
        for d in range(1, count):
            copy = pltpu.make_async_remote_copy(
                src_ref=buf.at[slot],
                dst_ref=buf.at[slot],
                send_sem=send.at[d - 1],
                recv_sem=recv.at[d - 1],
                device_id=place(d),
                device_id_type=pl.DeviceIdType.MESH,
            )
            copy.start()
            out.append(copy)
        return out

    def receive(buf, slot, place, count, send, recv):
        for d in range(1, count):
            pltpu.make_async_remote_copy(
                src_ref=buf.at[slot],
                dst_ref=buf.at[(slot + count - d) % count],
                send_sem=send.at[d - 1],
                recv_sem=recv.at[d - 1],
                device_id=place(d),
                device_id_type=pl.DeviceIdType.MESH,
            ).wait_recv()

    def climb(buf, bits, which, first):
        lifted = [unpack(buf[i]) for i in range(2**bits)]
        for step in range(bits):
            at, count, level, _ = spans[first + step]
            grams = [lifted[2 * i] + lifted[2 * i + 1] for i in range(count)]
            for i in range(count):
                total_at = path_slots.at[i]
                total_at[...] = grams[i]
            path_rows.append(None)
            chosen = path_slots[which >> (step + 1)]
            slot = first + step
            if slot % 2 == 0:
                path[slot // 2, :, :RANK] = chosen
            else:
                path[slot // 2, :, RANK:] = chosen
            if level > 0:
                fetches[first + step].wait()
                edge[first + step + 1] = nodes[at + (which >> (step + 1))]
                lifted = [lift(grams[i], nodes[at + i]) for i in range(count)]
        return lifted[0]

    path_slots = mine.at[pl.ds(0, 4)]
    path_rows = []

    out = sends(row_buf, row_id, to_row, n_rows, row_send, row_recv)
    eliminate(state, pairs + 1, 0, 8)
    receive(row_buf, row_id, to_row, n_rows, row_send, row_recv)
    z_buf[z_id] = pack(climb(row_buf, row_bits, row_id, 0))
    out += sends(z_buf, z_id, to_z, n_z, z_send, z_recv)
    eliminate(state, pairs + 1, 8, 40)
    receive(z_buf, z_id, to_z, n_z, z_send, z_recv)
    x_buf[x_id] = pack(climb(z_buf, Z_BITS, z_id, row_bits))
    out += sends(x_buf, x_id, to_x, n_x, x_send, x_recv)
    eliminate(state, pairs + 1, 40, RANK)
    own_upper, _ = triangles(state[pairs][:, :RANK])
    lows[x_id, z_id] = pack(own_upper)

    for d in range(1, n_z):
        copy = pltpu.make_async_remote_copy(
            src_ref=lows.at[x_id, z_id],
            dst_ref=lows.at[x_id, z_id],
            send_sem=zl_send.at[d - 1],
            recv_sem=zl_recv.at[d - 1],
            device_id=to_z(d),
            device_id_type=pl.DeviceIdType.MESH,
        )
        copy.start()
        out.append(copy)
    receive(x_buf, x_id, to_x, n_x, x_send, x_recv)
    climb(x_buf, x_bits, x_id, row_bits + Z_BITS)
    for d in range(1, n_z):
        pltpu.make_async_remote_copy(
            src_ref=lows.at[x_id, z_id],
            dst_ref=lows.at[x_id, (z_id + n_z - d) % n_z],
            send_sem=zl_send.at[d - 1],
            recv_sem=zl_recv.at[d - 1],
            device_id=to_z(d),
            device_id_type=pl.DeviceIdType.MESH,
        ).wait_recv()
    out += sends(lows, x_id, to_x, n_x, xl_send, xl_recv)
    eliminate(path, levels // 2, 0, RANK)
    for p in range(pairs + 1):
        leaf_out[p] = state[p]
    path_out[...] = path[...]
    edge_out[...] = edge[...]
    receive(lows, x_id, to_x, n_x, xl_send, xl_recv)
    for x in range(n_x):
        for z in range(n_z):
            low_out[x * n_z + z] = lows[x, z]
    for copy in out:
        copy.wait_send()


def finish_kernel(
    row_bits, levels, step_leaves,
    offsets, basis, transfer, couplings, leaf_state, own_state, path, edge, lows,
    orth_out, bridge_out, trans_out, coupled_out,
    own_upper, own_inverse,
):
    step = pl.program_id(0)
    n_leaf = lows.shape[0]
    branch = lax.axis_index("leaf")

    @pl.when(step == 0)
    def _():
        upper, inverse = triangles(own_state[0][:, :RANK])
        own_upper[...] = upper
        own_inverse[...] = inverse
        for k in range(levels):
            h = (k % 2) * RANK
            above, above_inverse = triangles(path[k // 2][:, h : h + RANK])
            trans_out[0, k] = mm(mm(upper, edge[k]), above_inverse, "nt")
            upper = above

    for i in range(step_leaves):
        h = (i % 2) * RANK
        upper, inverse = triangles(leaf_state[i // 2][:, h : h + RANK])
        orth_out[i] = mm(inverse, basis[i])
        bridge_out[i] = mm(mm(upper, transfer[i]), own_inverse[...], "nt")
        offset = offsets[step * step_leaves + i]
        column = (branch + offset // (2**row_bits)) % n_leaf
        low = unpack(lows[column])
        coupled_out[i] = mm(own_upper[...], mm(couplings[i], low, "nt"))


def per_device(
    leaf_basis, leaf_transfer, device_transfer, upper_transfer, couplings, couple_offset
):
    n_rows = lax.axis_size("rows")
    n_leaf = lax.axis_size("leaf")
    row_bits = n_rows.bit_length() - 1
    x_bits = n_leaf.bit_length() - 1 - Z_BITS
    n_z, n_x = 2**Z_BITS, 2**x_bits
    levels = row_bits + Z_BITS + x_bits
    leaves, _, width = leaf_basis.shape
    pairs = leaves // 2
    f32 = jnp.float32
    vmem = pl.BlockSpec(memory_space=pltpu.VMEM)
    n_nodes = n_rows - 1 + n_z - 1 + n_x - 1
    dma = pltpu.SemaphoreType.DMA
    half = RANK // 2
    leaf_state, path, lows, edge = pl.pallas_call(
        functools.partial(tree_kernel, row_bits, x_bits),
        out_shape=(
            jax.ShapeDtypeStruct((pairs + 1, RANK, 128), f32),
            jax.ShapeDtypeStruct((levels // 2, RANK, 128), f32),
            jax.ShapeDtypeStruct((n_leaf, half, 128), f32),
            jax.ShapeDtypeStruct((levels, RANK, RANK), f32),
        ),
        in_specs=[vmem, vmem, vmem, pl.BlockSpec(memory_space=pl.ANY)],
        out_specs=(vmem, vmem, vmem, vmem),
        scratch_shapes=[
            pltpu.VMEM((pairs + 1, RANK, 128), f32),
            pltpu.VMEM((levels // 2, RANK, 128), f32),
            pltpu.VMEM((levels, RANK, RANK), f32),
            pltpu.VMEM((n_nodes, RANK, RANK), f32),
            pltpu.VMEM((RANK, RANK), f32),
            pltpu.VMEM((n_rows, half, 128), f32),
            pltpu.VMEM((n_z, half, 128), f32),
            pltpu.VMEM((n_x, half, 128), f32),
            pltpu.VMEM((n_x, n_z, half, 128), f32),
            pltpu.VMEM((4, RANK, RANK), f32),
            dma((levels,)),
            dma((n_rows - 1,)), dma((n_rows - 1,)),
            dma((n_z - 1,)), dma((n_z - 1,)),
            dma((n_x - 1,)), dma((n_x - 1,)),
            dma((n_z - 1,)), dma((n_z - 1,)),
            dma((n_x - 1,)), dma((n_x - 1,)),
        ],
        compiler_params=pltpu.CompilerParams(
            collective_id=0, has_side_effects=True, vmem_limit_bytes=40 * 2**20
        ),
    )(leaf_basis, leaf_transfer, device_transfer, upper_transfer)

    chunk = 8
    full = lambda *shape: pl.BlockSpec(shape, lambda i: (0,) * len(shape))
    part = lambda *shape: pl.BlockSpec(shape, lambda i: (i,) + (0,) * (len(shape) - 1))
    return pl.pallas_call(
        functools.partial(finish_kernel, row_bits, levels, chunk),
        grid=(leaves // chunk,),
        out_shape=(
            jax.ShapeDtypeStruct((leaves, RANK, width), f32),
            jax.ShapeDtypeStruct((leaves, RANK, RANK), f32),
            jax.ShapeDtypeStruct((1, levels, RANK, RANK), f32),
            jax.ShapeDtypeStruct((leaves, RANK, RANK), f32),
        ),
        in_specs=[
            pl.BlockSpec(memory_space=pltpu.SMEM),
            part(chunk, RANK, width),
            part(chunk, RANK, RANK),
            part(chunk, RANK, RANK),
            part(chunk // 2, RANK, 128),
            pl.BlockSpec((1, RANK, 128), lambda i: (pairs, 0, 0)),
            full(levels // 2, RANK, 128),
            full(levels, RANK, RANK),
            full(n_leaf, half, 128),
        ],
        out_specs=(
            part(chunk, RANK, width),
            part(chunk, RANK, RANK),
            full(1, levels, RANK, RANK),
            part(chunk, RANK, RANK),
        ),
        scratch_shapes=[pltpu.VMEM((RANK, RANK), f32), pltpu.VMEM((RANK, RANK), f32)],
        compiler_params=pltpu.CompilerParams(vmem_limit_bytes=40 * 2**20),
    )(couple_offset, leaf_basis, leaf_transfer, couplings, leaf_state, leaf_state, path, edge, lows)


def solution(mesh):
    split = P(("leaf", "rows"))
    return jax.shard_map(
        per_device,
        mesh=mesh,
        in_specs=(split, split, split, P(), split, split),
        out_specs=(split, split, split, split),
        check_vma=False,
    )
```

time: 837 us -> 81.6 us (0.10); the launches traced: 827 us -> 80.2 us
  other arithmetic: 625 us -> 0 us
  local copies, waits for them, and re-layouts: 99.8 us -> 11.6 us
  Pallas kernels: 0 us -> 67.9 us
  matrix products: 37.7 us -> 0 us
  blocking collectives: 25.8 us -> 0 us
  starting transfers between devices: 15.8 us -> 0 us
  between operations: 14.7 us -> 0.69 us
    another operation x18 -> x0, other arithmetic: 615 us -> none  [the longest x4 191 us: per_device(): leaf_low = jnp.linalg.cholesky(leaf_gram)]
    pallas_call x0 -> x2, Pallas kernels: none -> 67.9 us  [the longest x1 54.3 us: per_device(): pl.pallas_call(functools.partial(tree_kernel, row_bits, x_bits), out_shap...]
    unnamed x56 -> x13, local copies, waits for them, and re-layouts: 52.4 us -> 11.6 us
    dot_general x24 -> x0, matrix products: 29.6 us -> none  [the longest x9 6.56 us: lift(): inner = jnp.einsum('nkl,nlj->nkj', grams, trans, precision=HIGH)]
    dynamic_slice x3 -> x0, local copies, waits for them, and re-layouts: 26.7 us -> none  [the longest x1 18.5 us: per_device(): lax.dynamic_index_in_dim(upper_transfer, 2 ** node_level - 2 + (myself >>...]
    all_gather x2 -> x0, blocking collectives: 25.8 us -> none  [the longest x1 13 us: per_device(): lax.all_gather(own_lift, 'rows', axis=0, tiled=True)]
    ppermute x5 -> x0, starting transfers between devices: 15.8 us -> none  [swapped(): return lax.ppermute(value, axis, pairs)]
    another operation x5 -> x0, local copies, waits for them, and re-layouts: 10.6 us -> none  [the longest x2 7.87 us: lower_solve(): return lax.linalg.triangular_solve(low, right, left_side=True, lower=True)]
  transfers between devices with their start and end apart: 6 -> 0, of which waited for: 4 -> 0; matrix products, arithmetic and copies ran while one was open for 61% -> 0% of each run, Pallas kernels for 0% -> 0%
where the time goes in v1:
time: 81.6 us; the launch traced here: 80.2 us
  Pallas kernels  67.9 us (83%)
  local copies, waits for them, and re-layouts  11.6 us (14%)
    pallas_call x1, Pallas kernels, per_device(): pl.pallas_call(functools.partial(tree_kernel, row_bits, x_bits), out_shap...  54.3 us
    pallas_call x1, Pallas kernels, per_device(): pl.pallas_call(functools.partial(finish_kernel, row_bits, levels, chunk),...  13.6 us
    unnamed x13, local copies, waits for them, and re-layouts  11.6 us

profile of v1, /device:TPU:8, one launch (start us, length us, event | category | flops | bytes accessed | tf_op | source)
XLA Modules:
  0.0 80.2 jit_solution(10479918980143197336)
XLA Ops:
  0.6 0.0 copy-start.2
  0.6 0.0 copy-start.1
  0.7 0.0 copy-start.4
  0.7 8.2 %copy.10.upper_transfer = f32[254,64,64]{2,1,0:T(8,128)} copy(f32[254,64,64]{0,2,1:T(8,128)} %param.9) | data formatting | bytes 8323072 | tf_op args[3]
  8.9 0.0 copy-done.2
  8.9 0.0 copy-done.1
  8.9 0.0 copy-done.4
  8.9 0.0 copy-start
  8.9 3.4 %copy-done = f32[254,64,64]{2,1,0:T(8,128)S(1)} copy-done((f32[254,64,64]{2,1,0:T(8,128)S(1)}, f32[254,64,64]{2,1,0:T(8,128)}, u32[]{:S(2)}) %copy-start) | copy-done | bytes 4161560
  12.3 0.0 copy-start.3
  12.3 0.0 copy-start.5
  12.3 54.3 %shard_map.93 = (f32[17,64,128]{2,1,0:T(8,128)S(1)}, f32[4,64,128]{2,1,0:T(8,128)S(1)}, f32[32,32,128]{2,1,0:T(8,128)S(1)}, f32[8,64,64]{2,1,0:T(8,128)S(1)}) custom-call(f32[32,64,256]{2,1,0:T(8,128)S(1)} %copy-done.1, f32[32,64,64]{2,1,0:T(8,128)S(1)} %copy-done.2, f32[1,64,64]{2,1,0:T(8,128)S(1)} %copy-done.4, f32[254,64,64]{2,1,0:T(8,128)S(1)} %copy-done), custom_call_target="tpu_custom_call" | custom-call | tf_op jit(solution)/shard_map/pallas_call | solution.py:299
  66.6 0.0 copy-done.3
  66.6 0.0 copy-done.5
  66.6 13.6 %shard_map.94 = (f32[32,64,256]{2,1,0:T(8,128)}, f32[32,64,64]{2,1,0:T(8,128)}, f32[1,8,64,64]{3,2,1,0:T(8,128)}, f32[32,64,64]{2,1,0:T(8,128)}) custom-call(s32[32]{0:T(128)S(1)} %copy-done.5, f32[32,64,256]{2,1,0:T(8,128)S(1)} %copy-done.1, f32[32,64,64]{2,1,0:T(8,128)S(1)} %copy-done.2, f32[32,64,64]{2,1,0:T(8,128)S(1)} %copy-done.3, ...), custom_call_target="tpu_custom_call" | custom-call | tf_op jit(solution)/shard_map/pallas_call | solution.py:335
Async XLA Ops:
  0.6 8.3 %copy-start.2 = (f32[32,64,64]{2,1,0:T(8,128)S(1)}, f32[32,64,64]{2,1,0:T(8,128)}, u32[]{:S(2)}) copy-start(f32[32,64,64]{2,1,0:T(8,128)} %transfer.3) | copy-start | bytes 1572868
  0.6 8.3 %copy-start.1 = (f32[32,64,256]{2,1,0:T(8,128)S(1)}, f32[32,64,256]{2,1,0:T(8,128)}, u32[]{:S(2)}) copy-start(f32[32,64,256]{2,1,0:T(8,128)} %basis.3) | copy-start | bytes 6291460
  0.7 8.3 %copy-start.4 = (f32[1,64,64]{2,1,0:T(8,128)S(1)}, f32[1,64,64]{2,1,0:T(8,128)}, u32[]{:S(2)}) copy-start(f32[1,64,64]{2,1,0:T(8,128)} %device_transfer.1) | copy-start | bytes 49156
  8.9 3.4 %copy-start = (f32[254,64,64]{2,1,0:T(8,128)S(1)}, f32[254,64,64]{2,1,0:T(8,128)}, u32[]{:S(2)}) copy-start(f32[254,64,64]{2,1,0:T(8,128)} %copy.10.upper_transfer) | copy-start | bytes 12484612
  12.3 54.3 %copy-start.3 = (f32[32,64,64]{2,1,0:T(8,128)S(1)}, f32[32,64,64]{2,1,0:T(8,128)}, u32[]{:S(2)}) copy-start(f32[32,64,64]{2,1,0:T(8,128)} %couplings.1) | copy-start | bytes 1572868
  12.3 54.3 %copy-start.5 = (s32[32]{0:T(128)S(1)}, s32[32]{0:T(128)}, u32[]{:S(2)}) copy-start(s32[32]{0:T(128)} %offsets.1) | copy-start | bytes 388

commit v2 on v1

v2 whole, which is shorter than its diff:
```python
import functools

import jax
import jax.numpy as jnp
from jax import lax
from jax.experimental import pallas as pl
from jax.experimental.pallas import tpu as pltpu
from jax.sharding import PartitionSpec as P

HIGH = lax.Precision.HIGHEST
RANK = 64
HALF = 32
SLOTS = 128
NODES = 256
Z_BITS = 3


def mm(a, b, dims="nn"):
    contract = ((1 if dims[0] == "n" else 0,), (0 if dims[1] == "n" else 1,))
    return lax.dot_general(
        a, b, (contract, ((), ())), precision=HIGH, preferred_element_type=jnp.float32
    )


def lift(grams, trans):
    inner = [mm(g, t) for g, t in zip(grams, trans)]
    return [mm(t, i, "tn") for t, i in zip(trans, inner)]


def pack(a):
    return jnp.concatenate([a[:HALF], a[HALF:]], axis=1)


def unpack(a):
    return jnp.concatenate([a[:, :RANK], a[:, RANK:]], axis=0)


def slot(index):
    return pl.ds(index, HALF, stride=SLOTS)


def eliminate(x):
    sub = lax.broadcasted_iota(jnp.int32, (8, SLOTS), 0)
    group = 4
    for v in range(RANK // 8):
        base = 8 * v
        block = [x[base + t, base : base + 8, :] for t in range(8)]
        scales = []
        for t in range(8):
            scale = lax.rsqrt(jnp.broadcast_to(block[t][t : t + 1], (8, SLOTS)))
            row = jnp.where(sub == t, 1.0, block[t]) * scale
            x[base + t, base : base + 8, :] = row
            scales.append(scale[:1])
            for u in range(t + 1, 8):
                block[u] = jnp.where(sub == t, 0.0, block[u]) - row[u : u + 1] * row
        for lo, hi in ((0, base), (base + 8, RANK)):
            if lo == hi:
                continue
            rows = [x[base + t, lo:hi, :] for t in range(8)]
            for t in range(8):
                row = rows[t] * scales[t]
                x[base + t, lo:hi, :] = row
                for u in range(t + 1, 8):
                    rows[u] = rows[u] - x[base + t, base + u : base + u + 1, :] * row
        if base + 8 == RANK:
            break
        mid = [jnp.where(sub <= t, x[base + t, base : base + 8, :], 0.0) for t in range(8)]
        for later in range(v + 1, RANK // 8):

            def below(g, carry, base=base, later=later, mid=mid):
                first = 8 * later + g * group
                factor = [
                    [x[base + t, pl.ds(first + r, 1), :] for t in range(8)] for r in range(group)
                ]
                for lo, hi in ((0, base), (8 * later, RANK)):
                    for c in range(lo, hi, 8):
                        acc = [x[first + r, c : c + 8, :] for r in range(group)]
                        for t in range(8):
                            row = x[base + t, c : c + 8, :]
                            for r in range(group):
                                acc[r] = acc[r] - factor[r][t] * row
                        for r in range(group):
                            x[first + r, c : c + 8, :] = acc[r]
                for r in range(group):
                    acc = -(factor[r][0] * mid[0])
                    for t in range(1, 8):
                        acc = acc - factor[r][t] * mid[t]
                    x[first + r, base : base + 8, :] = acc
                return carry

            lax.fori_loop(0, 8 // group, below, 0)


def triangles(a):
    lane = lax.broadcasted_iota(jnp.int32, (HALF, 128), 1)
    row = lax.broadcasted_iota(jnp.int32, (HALF, 128), 0) + (lane // RANK) * HALF
    off = (lane & (RANK - 1)) - row
    parts = [a[8 * v : 8 * v + 8] for v in range(HALF // 8)]
    offs = [off[8 * v : 8 * v + 8] for v in range(HALF // 8)]
    diagonal = jnp.ones_like(parts[0])
    for part, o in zip(parts, offs):
        diagonal = jnp.where(o == 0, part, diagonal)
    diagonal = 1.0 / diagonal
    upper = [
        jnp.where(o > 0, part, jnp.where(o == 0, diagonal, 0.0)) for part, o in zip(parts, offs)
    ]
    inverse = [jnp.where(o <= 0, part, 0.0) for part, o in zip(parts, offs)]
    return jnp.concatenate(upper, axis=0), jnp.concatenate(inverse, axis=0)


def tree_kernel(
    row_bits, x_bits,
    basis_in, transfer_in, device_transfer, upper_in,
    factors_out, edge_out,
    basis, transfer, upper, nodes, total, grams, lanes, work,
    row_buf, z_buf, x_buf, cols,
    in_sem, row_send, row_recv, z_send, z_recv, x_send, x_recv,
    zl_send, zl_recv, xl_send, xl_recv,
):
    n_rows, n_z, n_x = 2**row_bits, 2**Z_BITS, 2**x_bits
    levels = row_bits + Z_BITS + x_bits
    branch = lax.axis_index("leaf")
    row_id = lax.axis_index("rows")
    x_id = branch // n_z
    z_id = branch % n_z
    leaves = basis.shape[0]
    columns = leaves
    paths = columns + n_x * n_z

    def to_row(d):
        return {"rows": (row_id + d) % n_rows}

    def to_z(d):
        return {"leaf": x_id * n_z + (z_id + d) % n_z}

    def to_x(d):
        return {"leaf": ((x_id + d) % n_x) * n_z + z_id}

    chunks = 4
    size = leaves // chunks
    fetch_transfer = pltpu.make_async_copy(transfer_in, transfer, in_sem.at[chunks])
    fetches = [
        pltpu.make_async_copy(
            basis_in.at[pl.ds(c * size, size)], basis.at[pl.ds(c * size, size)], in_sem.at[c]
        )
        for c in range(chunks)
    ]
    fetch_upper = pltpu.make_async_copy(upper_in, upper, in_sem.at[chunks + 1])
    fetches[0].start()
    fetch_transfer.start()
    for fetch in fetches[1:]:
        fetch.start()
    fetch_upper.start()

    barrier = pltpu.get_barrier_semaphore()
    for place, count in ((to_row, n_rows), (to_z, n_z), (to_x, n_x)):
        for d in range(1, count):
            pl.semaphore_signal(
                barrier, inc=1, device_id=place(d), device_id_type=pl.DeviceIdType.MESH
            )

    total[...] = jnp.zeros_like(total)

    batch = 8

    def leaf_group(g, carry):
        first = batch * g
        group = [mm(basis[first + h], basis[first + h], "nt") for h in range(batch)]
        moved = [mm(group[h], transfer[first + h]) for h in range(batch)]
        for h in range(batch):
            grams[slot(first + h), :] = pack(group[h])
        trans = transfer[pl.ds(first, batch)].reshape(batch * RANK, RANK)
        total[...] += mm(trans, jnp.concatenate(moved, axis=0), "tn")
        return carry

    fetch_transfer.wait()
    for c in range(chunks):
        fetches[c].wait()
        lax.fori_loop(c * size // batch, (c + 1) * size // batch, leaf_group, 0)
    own = total[...]
    edge_out[0] = pack(device_transfer[0])
    row_buf[row_id] = pack(lift([own], [device_transfer[0]])[0])
    pl.semaphore_wait(barrier, n_rows - 1 + n_z - 1 + n_x - 1)

    def sends(buf, at, place, count, send, recv):
        out = []
        for d in range(1, count):
            copy = pltpu.make_async_remote_copy(
                src_ref=buf.at[at],
                dst_ref=buf.at[at],
                send_sem=send.at[d - 1],
                recv_sem=recv.at[d - 1],
                device_id=place(d),
                device_id_type=pl.DeviceIdType.MESH,
            )
            copy.start()
            out.append(copy)
        return out

    def receive(buf, at, place, count, send, recv):
        for d in range(1, count):
            pltpu.make_async_remote_copy(
                src_ref=buf.at[at],
                dst_ref=buf.at[(at + count - d) % count],
                send_sem=send.at[d - 1],
                recv_sem=recv.at[d - 1],
                device_id=place(d),
                device_id_type=pl.DeviceIdType.MESH,
            ).wait_recv()

    def climb(buf, bits, which, level):
        lifted = [unpack(buf[i]) for i in range(2**bits)]
        for step in range(bits):
            level -= 1
            count = 2 ** (bits - 1 - step)
            own_node = which >> (step + 1)
            rise = [lifted[2 * i] + lifted[2 * i + 1] for i in range(count)]
            for i in range(count):
                work[i] = pack(rise[i])
            k = levels - 1 - level
            grams[slot(paths + k), :] = work[own_node]
            if level > 0:
                start = 2**level - 2 + ((row_id + n_rows * branch) >> (levels - level)) - own_node
                for i in range(count):
                    work[i] = nodes[pl.ds(start + i, HALF, stride=NODES), :]
                edge_out[k + 1] = work[own_node]
                lifted = lift(rise, [unpack(work[i]) for i in range(count)])
        return lifted[0]

    out = sends(row_buf, row_id, to_row, n_rows, row_send, row_recv)
    cols[x_id, z_id] = pack(own)
    for d in range(1, n_z):
        copy = pltpu.make_async_remote_copy(
            src_ref=cols.at[x_id, z_id],
            dst_ref=cols.at[x_id, z_id],
            send_sem=zl_send.at[d - 1],
            recv_sem=zl_recv.at[d - 1],
            device_id=to_z(d),
            device_id_type=pl.DeviceIdType.MESH,
        )
        copy.start()
        out.append(copy)

    fetch_upper.wait()

    def turn(r, carry):
        for lo, hi in ((0, 128), (128, upper.shape[2])):
            both = jnp.concatenate([upper[r, :, lo:hi], upper[HALF + r, :, lo:hi]], axis=0)
            nodes[pl.ds(r * NODES + lo, hi - lo), :] = both.T
        return carry

    lax.fori_loop(0, HALF, turn, 0, unroll=2)
    receive(row_buf, row_id, to_row, n_rows, row_send, row_recv)
    z_buf[z_id] = pack(climb(row_buf, row_bits, row_id, levels))
    out += sends(z_buf, z_id, to_z, n_z, z_send, z_recv)
    for d in range(1, n_z):
        pltpu.make_async_remote_copy(
            src_ref=cols.at[x_id, z_id],
            dst_ref=cols.at[x_id, (z_id + n_z - d) % n_z],
            send_sem=zl_send.at[d - 1],
            recv_sem=zl_recv.at[d - 1],
            device_id=to_z(d),
            device_id_type=pl.DeviceIdType.MESH,
        ).wait_recv()
    out += sends(cols, x_id, to_x, n_x, xl_send, xl_recv)
    receive(z_buf, z_id, to_z, n_z, z_send, z_recv)
    x_buf[x_id] = pack(climb(z_buf, Z_BITS, z_id, levels - row_bits))
    out += sends(x_buf, x_id, to_x, n_x, x_send, x_recv)
    receive(x_buf, x_id, to_x, n_x, x_send, x_recv)
    climb(x_buf, x_bits, x_id, x_bits)
    receive(cols, x_id, to_x, n_x, xl_send, xl_recv)
    for x in range(n_x):
        for z in range(n_z):
            grams[slot(columns + x * n_z + z), :] = cols[x, z]

    def to_lanes(r, carry):
        both = grams[pl.ds(pl.multiple_of(r * SLOTS, SLOTS), SLOTS), :].T
        lanes[r] = both[:RANK]
        lanes[HALF + r] = both[RANK:]
        return carry

    def from_lanes(r, carry):
        both = jnp.concatenate([lanes[r], lanes[HALF + r]], axis=0)
        factors_out[pl.ds(pl.multiple_of(r * SLOTS, SLOTS), SLOTS), :] = both.T
        return carry

    lax.fori_loop(0, HALF, to_lanes, 0, unroll=2)
    eliminate(lanes)
    lax.fori_loop(0, HALF, from_lanes, 0, unroll=2)
    for copy in out:
        copy.wait_send()


def finish_kernel(
    row_bits, levels, step_leaves, leaves, n_leaf,
    offsets, basis, transfer, couplings, factors, edge,
    orth_out, bridge_out, trans_out, coupled_out,
    own_upper, own_inverse,
):
    step = pl.program_id(0)
    branch = lax.axis_index("leaf")

    def factor(index):
        upper, inverse = triangles(factors[slot(index), :])
        return unpack(upper), unpack(inverse)

    @pl.when(step == 0)
    def _():
        upper, inverse = factor(leaves + branch)
        own_upper[...] = upper
        own_inverse[...] = inverse
        above = [factor(leaves + n_leaf + k) for k in range(levels)]
        uppers = [upper] + [a[0] for a in above]
        inner = [mm(uppers[k], unpack(edge[k])) for k in range(levels)]
        for k in range(levels):
            trans_out[0, k] = mm(inner[k], above[k][1], "nt")

    each = range(step_leaves)
    pairs = [factor(step * step_leaves + i) for i in each]
    for i in each:
        orth_out[i] = mm(pairs[i][1], basis[i])
    inner = [mm(pairs[i][0], transfer[i]) for i in each]
    lows = []
    for i in each:
        offset = offsets[step * step_leaves + i]
        column = (branch + offset // (2**row_bits)) % n_leaf
        lows.append(factor(leaves + column)[0])
    right = [mm(couplings[i], lows[i], "nt") for i in each]
    inverse = own_inverse[...]
    upper = own_upper[...]
    for i in each:
        bridge_out[i] = mm(inner[i], inverse, "nt")
    for i in each:
        coupled_out[i] = mm(upper, right[i])


def per_device(
    leaf_basis, leaf_transfer, device_transfer, upper_transfer, couplings, couple_offset
):
    n_rows = lax.axis_size("rows")
    n_leaf = lax.axis_size("leaf")
    row_bits = n_rows.bit_length() - 1
    x_bits = n_leaf.bit_length() - 1 - Z_BITS
    n_z, n_x = 2**Z_BITS, 2**x_bits
    levels = row_bits + Z_BITS + x_bits
    leaves, _, width = leaf_basis.shape
    f32 = jnp.float32
    vmem = pl.BlockSpec(memory_space=pltpu.VMEM)
    hbm = pl.BlockSpec(memory_space=pltpu.HBM)
    dma = pltpu.SemaphoreType.DMA
    upper = jnp.transpose(upper_transfer, (1, 2, 0))
    factors, edge = pl.pallas_call(
        functools.partial(tree_kernel, row_bits, x_bits),
        out_shape=(
            jax.ShapeDtypeStruct((HALF * SLOTS, 128), f32),
            jax.ShapeDtypeStruct((levels, HALF, 128), f32),
        ),
        in_specs=[hbm, hbm, vmem, hbm],
        out_specs=(vmem, vmem),
        scratch_shapes=[
            pltpu.VMEM(leaf_basis.shape, f32),
            pltpu.VMEM(leaf_transfer.shape, f32),
            pltpu.VMEM(upper.shape, f32),
            pltpu.VMEM((HALF * NODES, 128), f32),
            pltpu.VMEM((RANK, RANK), f32),
            pltpu.VMEM((HALF * SLOTS, 128), f32),
            pltpu.VMEM((RANK, RANK, SLOTS), f32),
            pltpu.VMEM((4, HALF, 128), f32),
            pltpu.VMEM((n_rows, HALF, 128), f32),
            pltpu.VMEM((n_z, HALF, 128), f32),
            pltpu.VMEM((n_x, HALF, 128), f32),
            pltpu.VMEM((n_x, n_z, HALF, 128), f32),
            dma((6,)),
            dma((n_rows - 1,)), dma((n_rows - 1,)),
            dma((n_z - 1,)), dma((n_z - 1,)),
            dma((n_x - 1,)), dma((n_x - 1,)),
            dma((n_z - 1,)), dma((n_z - 1,)),
            dma((n_x - 1,)), dma((n_x - 1,)),
        ],
        compiler_params=pltpu.CompilerParams(
            collective_id=0, has_side_effects=True, vmem_limit_bytes=60 * 2**20
        ),
    )(leaf_basis, leaf_transfer, device_transfer, upper)

    chunk = 8
    full = lambda *shape: pl.BlockSpec(shape, lambda i: (0,) * len(shape))
    part = lambda *shape: pl.BlockSpec(shape, lambda i: (i,) + (0,) * (len(shape) - 1))
    return pl.pallas_call(
        functools.partial(finish_kernel, row_bits, levels, chunk, leaves, n_leaf),
        grid=(leaves // chunk,),
        out_shape=(
            jax.ShapeDtypeStruct((leaves, RANK, width), f32),
            jax.ShapeDtypeStruct((leaves, RANK, RANK), f32),
            jax.ShapeDtypeStruct((1, levels, RANK, RANK), f32),
            jax.ShapeDtypeStruct((leaves, RANK, RANK), f32),
        ),
        in_specs=[
            pl.BlockSpec(memory_space=pltpu.SMEM),
            part(chunk, RANK, width),
            part(chunk, RANK, RANK),
            part(chunk, RANK, RANK),
            vmem,
            vmem,
        ],
        out_specs=(
            part(chunk, RANK, width),
            part(chunk, RANK, RANK),
            full(1, levels, RANK, RANK),
            part(chunk, RANK, RANK),
        ),
        scratch_shapes=[pltpu.VMEM((RANK, RANK), f32), pltpu.VMEM((RANK, RANK), f32)],
        compiler_params=pltpu.CompilerParams(vmem_limit_bytes=60 * 2**20),
    )(couple_offset, leaf_basis, leaf_transfer, couplings, factors, edge)


def solution(mesh):
    split = P(("leaf", "rows"))
    return jax.shard_map(
        per_device,
        mesh=mesh,
        in_specs=(split, split, split, P(), split, split),
        out_specs=(split, split, split, split),
        check_vma=False,
    )
```

time: 81.6 us -> 54.2 us (0.66)
  Pallas kernels: 67.9 us -> 52.5 us
  local copies, waits for them, and re-layouts: 11.6 us -> 0 us
    pallas_call x1, Pallas kernels: 54.3 us -> 41 us  [per_device(): pl.pallas_call(functools.partial(tree_kernel, row_bits, x_bits), out_shap...]
    unnamed x13 -> x0, local copies, waits for them, and re-layouts: 11.6 us -> none
    pallas_call x1, Pallas kernels: 13.6 us -> 11.5 us  [per_device(): pl.pallas_call(functools.partial(finish_kernel, row_bits, levels, chunk,...]
where the time goes in v2:
time: 54.2 us; the launch traced here: 53.1 us
  Pallas kernels  52.5 us (97%)
  between operations  0.64 us (1%)
    pallas_call x1, Pallas kernels, per_device(): pl.pallas_call(functools.partial(tree_kernel, row_bits, x_bits), out_shap...  41 us
    pallas_call x1, Pallas kernels, per_device(): pl.pallas_call(functools.partial(finish_kernel, row_bits, levels, chunk,...  11.5 us

profile of v2, /device:TPU:8, one launch (start us, length us, event | category | flops | bytes accessed | tf_op | source)
XLA Modules:
  0.0 53.1 jit_solution(2950666144353860289)
XLA Ops:
  0.6 41.0 %shard_map.93 = (f32[4096,128]{1,0:T(8,128)}, f32[8,32,128]{2,1,0:T(8,128)}) custom-call(f32[32,64,256]{2,1,0:T(8,128)} %basis.1, f32[32,64,64]{2,1,0:T(8,128)} %transfer.1, f32[1,64,64]{2,1,0:T(8,128)} %device_transfer.1, f32[64,64,254]{2,1,0:T(8,128)} %bitcast.1), custom_call_target="tpu_custom_call" | custom-call | tf_op jit(solution)/shard_map/pallas_call | solution.py:352
  41.7 11.5 %shard_map.94 = (f32[32,64,256]{2,1,0:T(8,128)}, f32[32,64,64]{2,1,0:T(8,128)}, f32[1,8,64,64]{3,2,1,0:T(8,128)}, f32[32,64,64]{2,1,0:T(8,128)}) custom-call(s32[32]{0:T(128)} %offsets.1, f32[32,64,256]{2,1,0:T(8,128)} %basis.1, f32[32,64,64]{2,1,0:T(8,128)} %transfer.1, f32[32,64,64]{2,1,0:T(8,128)} %couplings.1, f32[4096,128]{1,0:T(8,128)} %get-tuple-element.6.factors, ...), custom_call_target="tpu_custom_call" | custom-call | tf_op jit(solution)/shard_map/pallas_call | solution.py:388

commit v3 on v2

--- a/solution.py
+++ b/solution.py
@@ -7,19 +7,30 @@
 from jax.experimental.pallas import tpu as pltpu
 from jax.sharding import PartitionSpec as P
 
-HIGH = lax.Precision.HIGHEST
 RANK = 64
 HALF = 32
-SLOTS = 128
+LANES = 128
+SLOTS = 72
 NODES = 256
 Z_BITS = 3
 
 
-def mm(a, b, dims="nn"):
+def mm(a, b, dims="nn", precision=lax.Precision.HIGHEST):
     contract = ((1 if dims[0] == "n" else 0,), (0 if dims[1] == "n" else 1,))
     return lax.dot_general(
-        a, b, (contract, ((), ())), precision=HIGH, preferred_element_type=jnp.float32
+        a, b, (contract, ((), ())), precision=precision, preferred_element_type=jnp.float32
     )
+
+
+def split(a):
+    high = a.astype(jnp.bfloat16)
+    return high, (a - high.astype(jnp.float32)).astype(jnp.bfloat16)
+
+
+def mm3(a, b, dims="nn"):
+    (ah, al), (bh, bl) = (x if isinstance(x, tuple) else split(x) for x in (a, b))
+    one = lambda p, q: mm(p, q, dims, lax.Precision.DEFAULT)
+    return one(ah, bh) + (one(ah, bl) + one(al, bh))
 
 
 def lift(grams, trans):
@@ -40,14 +51,14 @@
 
 
 def eliminate(x):
-    sub = lax.broadcasted_iota(jnp.int32, (8, SLOTS), 0)
-    group = 4
+    sub = lax.broadcasted_iota(jnp.int32, (8, LANES), 0)
+    group = 8
     for v in range(RANK // 8):
         base = 8 * v
         block = [x[base + t, base : base + 8, :] for t in range(8)]
         scales = []
         for t in range(8):
-            scale = lax.rsqrt(jnp.broadcast_to(block[t][t : t + 1], (8, SLOTS)))
+            scale = lax.rsqrt(jnp.broadcast_to(block[t][t : t + 1], (8, LANES)))
             row = jnp.where(sub == t, 1.0, block[t]) * scale
             x[base + t, base : base + 8, :] = row
             scales.append(scale[:1])
@@ -112,9 +123,9 @@
     row_bits, x_bits,
     basis_in, transfer_in, device_transfer, upper_in,
     factors_out, edge_out,
-    basis, transfer, upper, nodes, total, grams, lanes, work,
+    basis, transfer, upper, nodes, grams, lanes, work,
     row_buf, z_buf, x_buf, cols,
-    in_sem, row_send, row_recv, z_send, z_recv, x_send, x_recv,
+    in_sem, out_sem, row_send, row_recv, z_send, z_recv, x_send, x_recv,
     zl_send, zl_recv, xl_send, xl_recv,
 ):
     n_rows, n_z, n_x = 2**row_bits, 2**Z_BITS, 2**x_bits
@@ -136,12 +147,12 @@
     def to_x(d):
         return {"leaf": ((x_id + d) % n_x) * n_z + z_id}
 
-    chunks = 4
-    size = leaves // chunks
+    starts = (0, leaves // 4, leaves // 2, leaves)
+    chunks = len(starts) - 1
     fetch_transfer = pltpu.make_async_copy(transfer_in, transfer, in_sem.at[chunks])
     fetches = [
         pltpu.make_async_copy(
-            basis_in.at[pl.ds(c * size, size)], basis.at[pl.ds(c * size, size)], in_sem.at[c]
+            basis_in.at[starts[c] : starts[c + 1]], basis.at[starts[c] : starts[c + 1]], in_sem.at[c]
         )
         for c in range(chunks)
     ]
@@ -150,7 +161,6 @@
     fetch_transfer.start()
     for fetch in fetches[1:]:
         fetch.start()
-    fetch_upper.start()
 
     barrier = pltpu.get_barrier_semaphore()
     for place, count in ((to_row, n_rows), (to_z, n_z), (to_x, n_x)):
@@ -159,32 +169,30 @@
                 barrier, inc=1, device_id=place(d), device_id_type=pl.DeviceIdType.MESH
             )
 
-    total[...] = jnp.zeros_like(total)
-
-    batch = 8
-
-    def leaf_group(g, carry):
-        first = batch * g
+
+    def leaf_group(first, batch):
         group = [mm(basis[first + h], basis[first + h], "nt") for h in range(batch)]
+        if first == 0:
+            fetch_transfer.wait()
+            fetch_upper.start()
         moved = [mm(group[h], transfer[first + h]) for h in range(batch)]
         for h in range(batch):
             grams[slot(first + h), :] = pack(group[h])
-        trans = transfer[pl.ds(first, batch)].reshape(batch * RANK, RANK)
-        total[...] += mm(trans, jnp.concatenate(moved, axis=0), "tn")
-        return carry
-
-    fetch_transfer.wait()
+        trans = transfer[first : first + batch].reshape(batch * RANK, RANK)
+        return mm(trans, jnp.concatenate(moved, axis=0), "tn")
+
+    own = None
     for c in range(chunks):
         fetches[c].wait()
-        lax.fori_loop(c * size // batch, (c + 1) * size // batch, leaf_group, 0)
-    own = total[...]
+        part = leaf_group(starts[c], starts[c + 1] - starts[c])
+        own = part if own is None else own + part
     edge_out[0] = pack(device_transfer[0])
     row_buf[row_id] = pack(lift([own], [device_transfer[0]])[0])
     pl.semaphore_wait(barrier, n_rows - 1 + n_z - 1 + n_x - 1)
 
     def sends(buf, at, place, count, send, recv):
         out = []
-        for d in range(1, count):
+        for d in sorted(range(1, count), key=lambda d: -min(d, count - d)):
             copy = pltpu.make_async_remote_copy(
                 src_ref=buf.at[at],
                 dst_ref=buf.at[at],
@@ -209,14 +217,19 @@
             ).wait_recv()
 
     def climb(buf, bits, which, level):
-        lifted = [unpack(buf[i]) for i in range(2**bits)]
+        lifted = None
         for step in range(bits):
             level -= 1
             count = 2 ** (bits - 1 - step)
             own_node = which >> (step + 1)
-            rise = [lifted[2 * i] + lifted[2 * i + 1] for i in range(count)]
+            if step == 0:
+                packed = [buf[2 * i] + buf[2 * i + 1] for i in range(count)]
+                rise = [unpack(p) for p in packed]
+            else:
+                rise = [lifted[2 * i] + lifted[2 * i + 1] for i in range(count)]
+                packed = [pack(r) for r in rise]
             for i in range(count):
-                work[i] = pack(rise[i])
+                work[i] = packed[i]
             k = levels - 1 - level
             grams[slot(paths + k), :] = work[own_node]
             if level > 0:
@@ -249,7 +262,7 @@
             nodes[pl.ds(r * NODES + lo, hi - lo), :] = both.T
         return carry
 
-    lax.fori_loop(0, HALF, turn, 0, unroll=2)
+    lax.fori_loop(0, HALF, turn, 0, unroll=4)
     receive(row_buf, row_id, to_row, n_rows, row_send, row_recv)
     z_buf[z_id] = pack(climb(row_buf, row_bits, row_id, levels))
     out += sends(z_buf, z_id, to_z, n_z, z_send, z_recv)
@@ -273,20 +286,33 @@
         for z in range(n_z):
             grams[slot(columns + x * n_z + z), :] = cols[x, z]
 
+    def rows_of(r):
+        return pl.ds(pl.multiple_of(r * SLOTS, 8), SLOTS)
+
     def to_lanes(r, carry):
-        both = grams[pl.ds(pl.multiple_of(r * SLOTS, SLOTS), SLOTS), :].T
-        lanes[r] = both[:RANK]
-        lanes[HALF + r] = both[RANK:]
+        both = grams[rows_of(r), :].T
+        lanes[r, :, :SLOTS] = both[:RANK]
+        lanes[HALF + r, :, :SLOTS] = both[RANK:]
         return carry
 
     def from_lanes(r, carry):
-        both = jnp.concatenate([lanes[r], lanes[HALF + r]], axis=0)
-        factors_out[pl.ds(pl.multiple_of(r * SLOTS, SLOTS), SLOTS), :] = both.T
+        both = jnp.concatenate([lanes[r, :, :SLOTS], lanes[HALF + r, :, :SLOTS]], axis=0)
+        grams[rows_of(r), :] = both.T
         return carry
 
-    lax.fori_loop(0, HALF, to_lanes, 0, unroll=2)
+    lax.fori_loop(0, HALF, to_lanes, 0, unroll=4)
     eliminate(lanes)
-    lax.fori_loop(0, HALF, from_lanes, 0, unroll=2)
+    parts = 4
+    leave = []
+    for part in range(parts):
+        size = HALF // parts
+        lax.fori_loop(part * size, (part + 1) * size, from_lanes, 0, unroll=4)
+        span = pl.ds(part * size * SLOTS, size * SLOTS)
+        copy = pltpu.make_async_copy(grams.at[span], factors_out.at[span], out_sem.at[part])
+        copy.start()
+        leave.append(copy)
+    for copy in leave:
+        copy.wait()
     for copy in out:
         copy.wait_send()
 
@@ -311,27 +337,27 @@
         own_inverse[...] = inverse
         above = [factor(leaves + n_leaf + k) for k in range(levels)]
         uppers = [upper] + [a[0] for a in above]
-        inner = [mm(uppers[k], unpack(edge[k])) for k in range(levels)]
+        inner = [mm3(uppers[k], unpack(edge[k]), "nn") for k in range(levels)]
         for k in range(levels):
-            trans_out[0, k] = mm(inner[k], above[k][1], "nt")
+            trans_out[0, k] = mm3(inner[k], above[k][1], "nt")
 
     each = range(step_leaves)
     pairs = [factor(step * step_leaves + i) for i in each]
     for i in each:
-        orth_out[i] = mm(pairs[i][1], basis[i])
-    inner = [mm(pairs[i][0], transfer[i]) for i in each]
+        orth_out[i] = mm3(pairs[i][1], basis[i], "nn")
+    inner = [mm3(pairs[i][0], transfer[i], "nn") for i in each]
     lows = []
     for i in each:
         offset = offsets[step * step_leaves + i]
         column = (branch + offset // (2**row_bits)) % n_leaf
         lows.append(factor(leaves + column)[0])
-    right = [mm(couplings[i], lows[i], "nt") for i in each]
-    inverse = own_inverse[...]
-    upper = own_upper[...]
+    right = [mm3(couplings[i], lows[i], "nt") for i in each]
+    inverse = split(own_inverse[...])
+    upper = split(own_upper[...])
     for i in each:
-        bridge_out[i] = mm(inner[i], inverse, "nt")
+        bridge_out[i] = mm3(inner[i], inverse, "nt")
     for i in each:
-        coupled_out[i] = mm(upper, right[i])
+        coupled_out[i] = mm3(upper, right[i], "nn")
 
 
 def per_device(
@@ -356,21 +382,20 @@
             jax.ShapeDtypeStruct((levels, HALF, 128), f32),
         ),
         in_specs=[hbm, hbm, vmem, hbm],
-        out_specs=(vmem, vmem),
+        out_specs=(hbm, vmem),
         scratch_shapes=[
             pltpu.VMEM(leaf_basis.shape, f32),
             pltpu.VMEM(leaf_transfer.shape, f32),
             pltpu.VMEM(upper.shape, f32),
             pltpu.VMEM((HALF * NODES, 128), f32),
-            pltpu.VMEM((RANK, RANK), f32),
             pltpu.VMEM((HALF * SLOTS, 128), f32),
-            pltpu.VMEM((RANK, RANK, SLOTS), f32),
+            pltpu.VMEM((RANK, RANK, LANES), f32),
             pltpu.VMEM((4, HALF, 128), f32),
             pltpu.VMEM((n_rows, HALF, 128), f32),
             pltpu.VMEM((n_z, HALF, 128), f32),
             pltpu.VMEM((n_x, HALF, 128), f32),
             pltpu.VMEM((n_x, n_z, HALF, 128), f32),
-            dma((6,)),
+            dma((5,)), dma((4,)),
             dma((n_rows - 1,)), dma((n_rows - 1,)),
             dma((n_z - 1,)), dma((n_z - 1,)),
             dma((n_x - 1,)), dma((n_x - 1,)),

time: 54.2 us -> 45.1 us (0.83); the launches traced: 53.1 us -> 44.9 us
  Pallas kernels: 52.5 us -> 44.3 us
    pallas_call x1, Pallas kernels: 41 us -> 36.4 us  [per_device(): pl.pallas_call(functools.partial(tree_kernel, row_bits, x_bits), out_shap...]
    pallas_call x1, Pallas kernels: 11.5 us -> 7.86 us  [per_device(): pl.pallas_call(functools.partial(finish_kernel, row_bits, levels, chunk,...]
where the time goes in v3:
time: 45.1 us; the launch traced here: 44.9 us
  Pallas kernels  44.3 us (98%)
  between operations  0.64 us (1%)
    pallas_call x1, Pallas kernels, per_device(): pl.pallas_call(functools.partial(tree_kernel, row_bits, x_bits), out_shap...  36.4 us
    pallas_call x1, Pallas kernels, per_device(): pl.pallas_call(functools.partial(finish_kernel, row_bits, levels, chunk,...  7.86 us

profile of v3, /device:TPU:8, one launch (start us, length us, event | category | flops | bytes accessed | tf_op | source)
XLA Modules:
  0.0 44.9 jit_solution(13964944939735343892)
XLA Ops:
  0.6 36.4 %shard_map.93 = (f32[2304,128]{1,0:T(8,128)}, f32[8,32,128]{2,1,0:T(8,128)}) custom-call(f32[32,64,256]{2,1,0:T(8,128)} %basis.1, f32[32,64,64]{2,1,0:T(8,128)} %transfer.1, f32[1,64,64]{2,1,0:T(8,128)} %device_transfer.1, f32[64,64,254]{2,1,0:T(8,128)} %bitcast.1), custom_call_target="tpu_custom_call" | custom-call | tf_op jit(solution)/shard_map/pallas_call | solution.py:378
  37.0 7.9 %shard_map.94 = (f32[32,64,256]{2,1,0:T(8,128)}, f32[32,64,64]{2,1,0:T(8,128)}, f32[1,8,64,64]{3,2,1,0:T(8,128)}, f32[32,64,64]{2,1,0:T(8,128)}) custom-call(s32[32]{0:T(128)} %offsets.1, f32[32,64,256]{2,1,0:T(8,128)} %basis.1, f32[32,64,64]{2,1,0:T(8,128)} %transfer.1, f32[32,64,64]{2,1,0:T(8,128)} %couplings.1, f32[2304,128]{1,0:T(8,128)} %get-tuple-element.6.factors, ...), custom_call_target="tpu_custom_call" | custom-call | tf_op jit(solution)/shard_map/pallas_call | solution.py:413

commit v4 on v3

--- a/solution.py
+++ b/solution.py
@@ -156,11 +156,21 @@
         )
         for c in range(chunks)
     ]
-    fetch_upper = pltpu.make_async_copy(upper_in, upper, in_sem.at[chunks + 1])
+    quarter = RANK // 4
+    fetch_upper = [
+        pltpu.make_async_copy(
+            upper_in.at[pl.ds(q * quarter, quarter)],
+            upper.at[pl.ds(q * quarter, quarter)],
+            in_sem.at[chunks + 1 + q],
+        )
+        for q in range(4)
+    ]
     fetches[0].start()
     fetch_transfer.start()
-    for fetch in fetches[1:]:
+    fetches[1].start()
+    for fetch in fetch_upper:
         fetch.start()
+    fetches[2].start()
 
     barrier = pltpu.get_barrier_semaphore()
     for place, count in ((to_row, n_rows), (to_z, n_z), (to_x, n_x)):
@@ -174,16 +184,25 @@
         group = [mm(basis[first + h], basis[first + h], "nt") for h in range(batch)]
         if first == 0:
             fetch_transfer.wait()
-            fetch_upper.start()
         moved = [mm(group[h], transfer[first + h]) for h in range(batch)]
         for h in range(batch):
             grams[slot(first + h), :] = pack(group[h])
         trans = transfer[first : first + batch].reshape(batch * RANK, RANK)
         return mm(trans, jnp.concatenate(moved, axis=0), "tn")
 
+    def turn(r):
+        for lo, hi in ((0, 128), (128, upper.shape[2])):
+            both = jnp.concatenate([upper[r, :, lo:hi], upper[HALF + r, :, lo:hi]], axis=0)
+            nodes[r * NODES + lo : r * NODES + hi, :] = both.T
+
     own = None
     for c in range(chunks):
         fetches[c].wait()
+        if c == chunks - 1:
+            for fetch in fetch_upper:
+                fetch.wait()
+            for r in range(HALF):
+                turn(r)
         part = leaf_group(starts[c], starts[c + 1] - starts[c])
         own = part if own is None else own + part
     edge_out[0] = pack(device_transfer[0])
@@ -254,15 +273,6 @@
         copy.start()
         out.append(copy)
 
-    fetch_upper.wait()
-
-    def turn(r, carry):
-        for lo, hi in ((0, 128), (128, upper.shape[2])):
-            both = jnp.concatenate([upper[r, :, lo:hi], upper[HALF + r, :, lo:hi]], axis=0)
-            nodes[pl.ds(r * NODES + lo, hi - lo), :] = both.T
-        return carry
-
-    lax.fori_loop(0, HALF, turn, 0, unroll=4)
     receive(row_buf, row_id, to_row, n_rows, row_send, row_recv)
     z_buf[z_id] = pack(climb(row_buf, row_bits, row_id, levels))
     out += sends(z_buf, z_id, to_z, n_z, z_send, z_recv)
@@ -300,21 +310,21 @@
         grams[rows_of(r), :] = both.T
         return carry
 
-    lax.fori_loop(0, HALF, to_lanes, 0, unroll=4)
+    lax.fori_loop(0, HALF, to_lanes, 0, unroll=8)
     eliminate(lanes)
     parts = 4
     leave = []
     for part in range(parts):
         size = HALF // parts
-        lax.fori_loop(part * size, (part + 1) * size, from_lanes, 0, unroll=4)
+        lax.fori_loop(part * size, (part + 1) * size, from_lanes, 0, unroll=8)
         span = pl.ds(part * size * SLOTS, size * SLOTS)
         copy = pltpu.make_async_copy(grams.at[span], factors_out.at[span], out_sem.at[part])
         copy.start()
         leave.append(copy)
+    for copy in out:
+        copy.wait_send()
     for copy in leave:
         copy.wait()
-    for copy in out:
-        copy.wait_send()
 
 
 def finish_kernel(
@@ -395,7 +405,7 @@
             pltpu.VMEM((n_z, HALF, 128), f32),
             pltpu.VMEM((n_x, HALF, 128), f32),
             pltpu.VMEM((n_x, n_z, HALF, 128), f32),
-            dma((5,)), dma((4,)),
+            dma((8,)), dma((4,)),
             dma((n_rows - 1,)), dma((n_rows - 1,)),
             dma((n_z - 1,)), dma((n_z - 1,)),
             dma((n_x - 1,)), dma((n_x - 1,)),

time: 45.1 us -> 45.1 us (level)
  no operation moved by 1% of the time
where the time goes in v4:
time: 45.1 us; the launch traced here: 44.8 us
  Pallas kernels  44.2 us (98%)
  between operations  0.64 us (1%)
    pallas_call x1, Pallas kernels, per_device(): pl.pallas_call(functools.partial(tree_kernel, row_bits, x_bits), out_shap...  36.3 us
    pallas_call x1, Pallas kernels, per_device(): pl.pallas_call(functools.partial(finish_kernel, row_bits, levels, chunk,...  7.87 us

profile of v4, /device:TPU:8, one launch (start us, length us, event | category | flops | bytes accessed | tf_op | source)
XLA Modules:
  0.0 44.8 jit_solution(14116845333357621281)
XLA Ops:
  0.6 36.3 %shard_map.93 = (f32[2304,128]{1,0:T(8,128)}, f32[8,32,128]{2,1,0:T(8,128)}) custom-call(f32[32,64,256]{2,1,0:T(8,128)} %basis.1, f32[32,64,64]{2,1,0:T(8,128)} %transfer.1, f32[1,64,64]{2,1,0:T(8,128)} %device_transfer.1, f32[64,64,254]{2,1,0:T(8,128)} %bitcast.1), custom_call_target="tpu_custom_call" | custom-call | tf_op jit(solution)/shard_map/pallas_call | solution.py:388
  37.0 7.9 %shard_map.94 = (f32[32,64,256]{2,1,0:T(8,128)}, f32[32,64,64]{2,1,0:T(8,128)}, f32[1,8,64,64]{3,2,1,0:T(8,128)}, f32[32,64,64]{2,1,0:T(8,128)}) custom-call(s32[32]{0:T(128)} %offsets.1, f32[32,64,256]{2,1,0:T(8,128)} %basis.1, f32[32,64,64]{2,1,0:T(8,128)} %transfer.1, f32[32,64,64]{2,1,0:T(8,128)} %couplings.1, f32[2304,128]{1,0:T(8,128)} %get-tuple-element.6.factors, ...), custom_call_target="tpu_custom_call" | custom-call | tf_op jit(solution)/shard_map/pallas_call | solution.py:423

commit v5 on v4

--- a/solution.py
+++ b/solution.py
@@ -235,7 +235,23 @@
                 device_id_type=pl.DeviceIdType.MESH,
             ).wait_recv()
 
-    def climb(buf, bits, which, level):
+    def gather(bits, which, level):
+        trans = []
+        for step in range(bits):
+            level -= 1
+            if level > 0:
+                own = 2**level - 2 + ((row_id + n_rows * branch) >> (levels - level))
+                start = own - (which >> (step + 1))
+                edge_out[levels - level] = nodes[pl.ds(own, HALF, stride=NODES), :]
+                trans.append(
+                    [
+                        unpack(nodes[pl.ds(start + i, HALF, stride=NODES), :])
+                        for i in range(2 ** (bits - 1 - step))
+                    ]
+                )
+        return trans
+
+    def climb(buf, bits, which, level, trans):
         lifted = None
         for step in range(bits):
             level -= 1
@@ -252,11 +268,7 @@
             k = levels - 1 - level
             grams[slot(paths + k), :] = work[own_node]
             if level > 0:
-                start = 2**level - 2 + ((row_id + n_rows * branch) >> (levels - level)) - own_node
-                for i in range(count):
-                    work[i] = nodes[pl.ds(start + i, HALF, stride=NODES), :]
-                edge_out[k + 1] = work[own_node]
-                lifted = lift(rise, [unpack(work[i]) for i in range(count)])
+                lifted = lift(rise, trans[step])
         return lifted[0]
 
     out = sends(row_buf, row_id, to_row, n_rows, row_send, row_recv)
@@ -273,8 +285,9 @@
         copy.start()
         out.append(copy)
 
+    trans = gather(row_bits, row_id, levels)
     receive(row_buf, row_id, to_row, n_rows, row_send, row_recv)
-    z_buf[z_id] = pack(climb(row_buf, row_bits, row_id, levels))
+    z_buf[z_id] = pack(climb(row_buf, row_bits, row_id, levels, trans))
     out += sends(z_buf, z_id, to_z, n_z, z_send, z_recv)
     for d in range(1, n_z):
         pltpu.make_async_remote_copy(
@@ -286,11 +299,13 @@
             device_id_type=pl.DeviceIdType.MESH,
         ).wait_recv()
     out += sends(cols, x_id, to_x, n_x, xl_send, xl_recv)
+    trans = gather(Z_BITS, z_id, levels - row_bits)
     receive(z_buf, z_id, to_z, n_z, z_send, z_recv)
-    x_buf[x_id] = pack(climb(z_buf, Z_BITS, z_id, levels - row_bits))
+    x_buf[x_id] = pack(climb(z_buf, Z_BITS, z_id, levels - row_bits, trans))
     out += sends(x_buf, x_id, to_x, n_x, x_send, x_recv)
+    trans = gather(x_bits, x_id, x_bits)
     receive(x_buf, x_id, to_x, n_x, x_send, x_recv)
-    climb(x_buf, x_bits, x_id, x_bits)
+    climb(x_buf, x_bits, x_id, x_bits, trans)
     receive(cols, x_id, to_x, n_x, xl_send, xl_recv)
     for x in range(n_x):
         for z in range(n_z):

time: 45.1 us -> 44.6 us (0.989)
  Pallas kernels: 44.2 us -> 43.7 us
    pallas_call x1, Pallas kernels: 36.3 us -> 35.9 us  [per_device(): pl.pallas_call(functools.partial(tree_kernel, row_bits, x_bits), out_shap...]
where the time goes in v5:
time: 44.6 us; the launch traced here: 44.4 us
  Pallas kernels  43.7 us (98%)
  between operations  0.64 us (1%)
    pallas_call x1, Pallas kernels, per_device(): pl.pallas_call(functools.partial(tree_kernel, row_bits, x_bits), out_shap...  35.9 us
    pallas_call x1, Pallas kernels, per_device(): pl.pallas_call(functools.partial(finish_kernel, row_bits, levels, chunk,...  7.86 us

profile of v5, /device:TPU:8, one launch (start us, length us, event | category | flops | bytes accessed | tf_op | source)
XLA Modules:
  0.0 44.4 jit_solution(10193692648240076141)
XLA Ops:
  0.6 35.9 %shard_map.93 = (f32[2304,128]{1,0:T(8,128)}, f32[8,32,128]{2,1,0:T(8,128)}) custom-call(f32[32,64,256]{2,1,0:T(8,128)} %basis.1, f32[32,64,64]{2,1,0:T(8,128)} %transfer.1, f32[1,64,64]{2,1,0:T(8,128)} %device_transfer.1, f32[64,64,254]{2,1,0:T(8,128)} %bitcast.1), custom_call_target="tpu_custom_call" | custom-call | tf_op jit(solution)/shard_map/pallas_call | solution.py:403
  36.5 7.9 %shard_map.94 = (f32[32,64,256]{2,1,0:T(8,128)}, f32[32,64,64]{2,1,0:T(8,128)}, f32[1,8,64,64]{3,2,1,0:T(8,128)}, f32[32,64,64]{2,1,0:T(8,128)}) custom-call(s32[32]{0:T(128)} %offsets.1, f32[32,64,256]{2,1,0:T(8,128)} %basis.1, f32[32,64,64]{2,1,0:T(8,128)} %transfer.1, f32[32,64,64]{2,1,0:T(8,128)} %couplings.1, f32[2304,128]{1,0:T(8,128)} %get-tuple-element.6.factors, ...), custom_call_target="tpu_custom_call" | custom-call | tf_op jit(solution)/shard_map/pallas_call | solution.py:438
